TPU v7x, 512 devices: a whole 4x8x8 slice. The times are simulated.
512 devices in a mesh: dp: 16 (over y, core), tensor: 32 (over z, x).
Axes of the slice: x: 4, y: 8, z: 8, core: 2. Of those that a mesh axis runs over, the one named last changes fastest.
Arguments:
- tokens: bfloat16 [2048, 4096], P('dp', 'tensor'), may hold values from -6 to 6
- gate_pre: bfloat16 [2048, 16384], P('dp', 'tensor'), may hold values from -6 to 6
- up_blocks: bfloat16 [32, 64, 128, 128], P('tensor'), may hold values from -0.125 to 0.125
- up_mask: int32 [32, 128], P(None, 'tensor'), may hold values from 0 to 1, as said below
- down_blocks: bfloat16 [32, 64, 128, 128], P('tensor'), may hold values from -0.0625 to 0.0625
- down_mask: int32 [128, 32], replicated, may hold values from 0 to 1, as said below
- down_owner: int32 [128], replicated, may hold values from 0 to 31, as said below
- cotangent: bfloat16 [2048, 4096], P('dp', 'tensor'), may hold values from -6 to 6
Outputs:
- mixed: bfloat16 [2048, 4096], P('dp', 'tensor')
- input_grad: bfloat16 [2048, 4096], P('dp', 'tensor')
- gate_grad: bfloat16 [2048, 16384], P('dp', 'tensor')
- up_grad: bfloat16 [32, 64, 128, 128], P('tensor', 'dp')
- down_grad: bfloat16 [32, 64, 128, 128], P('tensor', 'dp')
Inputs may be any that keep to these rules, and one draw needn't show every extreme that they name: `up_mask`: each column strip of 4 block columns holds exactly 64 ones. `down_mask`: the rows owned by one device hold exactly 64 ones together. `down_owner`: every device owns exactly 4 block rows.
All inputs are finite; a program needn't handle non-finite values.
Results may differ from a plain program's by a relative error of at most 0.022.
Values may be sent and summed in bfloat16 or wider, within the bound.
No kernel may reach another device: no remote copies, remote signals or barrier semaphores. Data moves between devices by JAX's collectives and lax.ppermute only.
A program may use at most 128 MiB of HBM per device.

v0:
```python
import jax
import jax.numpy as jnp
from jax import lax
from jax.sharding import PartitionSpec as P


def kept_positions(marked, total):
    marked = marked.reshape(-1).astype(jnp.int32)
    running = jnp.cumsum(marked) - 1
    target = jnp.where(marked > 0, running, total)
    indices = jnp.arange(marked.shape[0], dtype=jnp.int32)
    return jnp.zeros((total,), jnp.int32).at[target].set(indices, mode="drop")


def one_hot(indices, total):
    return (indices[:, None] == jnp.arange(total, dtype=jnp.int32)[None, :]).astype(jnp.float32)


def row_slots(down_owner, devices):
    marks = (down_owner[:, None] == jnp.arange(devices, dtype=jnp.int32)[None, :]).astype(jnp.int32)
    earlier = jnp.cumsum(marks, axis=0) - marks
    return jnp.sum(earlier * marks, axis=1)


def picker(wanted, block, current, segment):
    block_count = segment.shape[1] // block
    inside = (wanted >= 0) & (wanted < block_count)
    shaped = segment.reshape(segment.shape[0], block_count, block)
    chosen = jnp.take(shaped, jnp.clip(wanted, 0, block_count - 1), axis=1)
    return jnp.where(inside[None, :, None], chosen, current)


def shards(tokens, gate_pre, up_blocks, up_mask, down_blocks, down_mask, down_owner, cotangent):
    devices = lax.axis_size("tensor")
    position = lax.axis_index("tensor")
    token_count = tokens.shape[0]
    blocks_wide = up_mask.shape[0]
    strip_size = up_mask.shape[1]
    block = up_blocks.shape[2]
    kept_up = up_blocks.shape[1]
    kept_down = down_blocks.shape[1]
    model_width = blocks_wide * block
    highest = lax.Precision.HIGHEST
    x_full, dy_full = (
        lax.all_gather(tokens, "tensor", axis=1, tiled=True),
        lax.all_gather(cotangent, "tensor", axis=1, tiled=True),
    )
    token_blocks = x_full.reshape(token_count, blocks_wide, block)
    cot_blocks = dy_full.reshape(token_count, blocks_wide, block)
    w_up = up_blocks[0]
    w_down = down_blocks[0]
    up_pos = kept_positions(up_mask, kept_up)
    up_rows = up_pos // strip_size
    up_cols = up_pos % strip_size
    token_chosen = jnp.take(token_blocks, up_rows, axis=1)
    product = jnp.einsum("nkb,kbc->nkc", token_chosen, w_up, preferred_element_type=jnp.float32)
    up_val = jnp.einsum("nkc,ks->nsc", product, one_hot(up_cols, strip_size), precision=highest)
    gate_val = gate_pre.reshape(token_count, strip_size, block).astype(jnp.float32)
    sigmoid_gate = jax.nn.sigmoid(gate_val)
    activated = gate_val * sigmoid_gate
    hidden = (activated * up_val).astype(jnp.bfloat16).reshape(token_count, strip_size * block)
    my_rows = kept_positions(down_owner == position, strip_size)
    owned_mask = jnp.take(down_mask, my_rows, axis=0)
    down_pos = kept_positions(owned_mask, kept_down)
    slots = down_pos // blocks_wide
    down_cols = down_pos % blocks_wide
    empty = jnp.zeros((token_count, strip_size, block), jnp.bfloat16)
    hidden_owned = picker(
        my_rows, block, empty, lax.all_gather(hidden, "tensor", axis=1, tiled=True)
    )
    h_chosen = jnp.take(hidden_owned, slots, axis=1)
    product = jnp.einsum("nkb,kbc->nkc", h_chosen, w_down, preferred_element_type=jnp.float32)
    out_part = jnp.einsum(
        "nkc,kj->njc", product, one_hot(down_cols, blocks_wide), precision=highest
    )
    out_part = out_part.astype(jnp.bfloat16).reshape(1, token_count, model_width)
    dy_chosen = jnp.take(cot_blocks, down_cols, axis=1)
    down_term = jnp.einsum("nkb,nkc->kbc", h_chosen, dy_chosen, preferred_element_type=jnp.float32)[
        None
    ]
    backward = jnp.einsum("nkc,kbc->nkb", dy_chosen, w_down, preferred_element_type=jnp.float32)
    dh_owned = jnp.einsum("nkb,ka->nab", backward, one_hot(slots, strip_size), precision=highest)
    dh_owned = dh_owned.astype(jnp.bfloat16).reshape(token_count, strip_size * block)
    home_index = down_owner * strip_size + row_slots(down_owner, devices)
    targets = position * strip_size + jnp.arange(strip_size, dtype=jnp.int32)
    wanted = jnp.take(home_index, targets)
    hidden_grad = picker(
        wanted, block, empty, lax.all_gather(dh_owned, "tensor", axis=1, tiled=True)
    )
    dh_float = hidden_grad.astype(jnp.float32)
    gate_grad = (dh_float * up_val * sigmoid_gate * (1.0 + gate_val * (1.0 - sigmoid_gate))).astype(
        jnp.bfloat16
    )
    gate_grad = gate_grad.reshape(token_count, strip_size * block)
    up_act_grad = (dh_float * activated).astype(jnp.bfloat16)
    du_chosen = jnp.take(up_act_grad, up_cols, axis=1)
    product = jnp.einsum("nkc,kbc->nkb", du_chosen, w_up, preferred_element_type=jnp.float32)
    in_part = jnp.einsum("nkb,kr->nrb", product, one_hot(up_rows, blocks_wide), precision=highest)
    in_part = in_part.astype(jnp.bfloat16).reshape(1, token_count, model_width)
    up_term = jnp.einsum(
        "nkb,nkc->kbc", token_chosen, du_chosen, preferred_element_type=jnp.float32
    )[None]
    out_pieces, in_pieces = (
        lax.all_to_all(out_part, "tensor", split_axis=2, concat_axis=0, tiled=True),
        lax.all_to_all(in_part, "tensor", split_axis=2, concat_axis=0, tiled=True),
    )
    mixed = jnp.sum(out_pieces.astype(jnp.float32), axis=0).astype(jnp.bfloat16)
    input_grad = jnp.sum(in_pieces.astype(jnp.float32), axis=0).astype(jnp.bfloat16)
    up_sum, down_sum = (
        lax.psum_scatter(
            up_term.astype(jnp.bfloat16), "dp", scatter_dimension=1, tiled=True
        ).astype(jnp.float32),
        lax.psum_scatter(
            down_term.astype(jnp.bfloat16), "dp", scatter_dimension=1, tiled=True
        ).astype(jnp.float32),
    )
    up_grad = up_sum.astype(jnp.bfloat16)
    down_grad = down_sum.astype(jnp.bfloat16)
    return (mixed, input_grad, gate_grad, up_grad, down_grad)


def solution(mesh):
    placed = (
        P("dp", "tensor"),
        P("dp", "tensor"),
        P("tensor", None, None, None),
        P(None, "tensor"),
        P("tensor", None, None, None),
        P(),
        P(),
        P("dp", "tensor"),
    )
    return jax.shard_map(
        shards,
        mesh=mesh,
        in_specs=placed,
        out_specs=(
            P("dp", "tensor"),
            P("dp", "tensor"),
            P("dp", "tensor"),
            P("tensor", "dp", None, None),
            P("tensor", "dp", None, None),
        ),
        check_vma=False,
    )
```

profile of v0, /device:TPU:2, one launch (start us, length us, event | category | flops | bytes accessed | tf_op | source)
XLA Modules:
  0.0 517.0 jit_solution(11576796951660111175)
XLA Ops:
  7.2 1.6 copy.130
  8.9 1.5 copy.121
  10.5 0.7 fusion.58
  11.2 0.7 fusion.72
  12.3 0.2 reduce_window_sum.22
  12.4 0.8 select_reduce_fusion
  13.3 0.7 multiply_add_fusion
  14.0 1.0 scatter_custom_fusion
  14.9 0.8 copy.115
  15.8 0.6 gather_fusion
  16.3 0.5 compare_and_fusion.8
  17.3 1.0 scatter_custom_fusion.1
  18.4 79.6 %all-gather.9.cloned.1.call-done = bf16[128,4096]{0,1:T(8,128)(2,1)} async-done(((bf16[128,128]{0,1:T(8,128)(2,1)}), bf16[128,4096]{0,1:T(8,128)(2,1)}) %all-gather.9.cloned.1.call-update) | async-done | bytes 1048592 | tf_op jit(solution)/shard_map/all_gather | solution.py:46
  98.0 1.6 copy.131
  99.6 2.2 gather_fusion.5
  101.8 3.8 convolution_bitcast_fusion.1
  105.7 3.8 fusion.48
  109.5 0.8 copy.146
  110.8 0.6 gather_fusion.1
  111.6 1.4 scatter_custom_fusion.2
  113.0 0.5 compare_and_fusion.6
  113.5 0.5 compare_and_fusion.1
  114.1 0.6 compare_and_fusion
  114.6 0.5 copy-done.13
  115.2 66.1 %all-gather.5.cloned.1.call-done = bf16[128,4096]{0,1:T(8,128)(2,1)} async-done(((bf16[128,128]{0,1:T(8,128)(2,1)}), bf16[128,4096]{0,1:T(8,128)(2,1)}) %all-gather.5.cloned.1.call-update) | async-done | bytes 1048592 | tf_op jit(solution)/shard_map/all_gather | solution.py:45
  181.2 1.6 copy.122
  182.9 2.2 gather_fusion.2
  185.0 4.3 convolution_bitcast_fusion.3
  189.4 80.9 %all-gather.11.cloned.1.call-done = bf16[128,16384]{0,1:T(8,128)(2,1)} async-done(((bf16[128,512]{0,1:T(8,128)(2,1)}), bf16[128,16384]{0,1:T(8,128)(2,1)}) %all-gather.11.cloned.1.call-update) | async-done | bytes 4194320 | tf_op jit(solution)/shard_map/all_gather | solution.py:88
  270.3 6.4 %copy.134 = bf16[128,128,128]{2,0,1:T(8,128)(2,1)} copy(bf16[128,128,128]{0,2,1:T(8,128)(2,1)} %bitcast.106) | data formatting | bytes 8388608 | tf_op jit(solution)/shard_map/reshape | solution.py:28
  276.7 2.8 gather_fusion.6
  279.4 6.0 %fusion.54 = (bf16[128,4,128]{2,1,0:T(4,128)(2,1)S(1)}, bf16[128,4,128]{2,1,0:T(4,128)(2,1)S(1)}, bf16[128,4,128]{2,1,0:T(4,128)(2,1)S(1)}) fusion(f32[128,4,128]{2,1,0:T(4,128)S(1)} %reshape.234, bf16[4,128,128]{2,1,0:T(8,128)(2,1)S(1)} %gather_fusion.6, pred[4]{0:T(512)(128)(4,1)S(1)} %copy-done.17, pred[4]{0:T(512)(128)(4,1)S(1)} %copy-done.16, ...), kind=kOutput, calls=%fused_computation.55 | convolution fusion | flops 51511552 | bytes 4981000 | tf_op jit(solution)/shard_map/nkc,ks->nsc/dot_general | solution.py:57
  285.5 0.8 copy.145
  286.4 2.2 gather_fusion.7
  288.6 4.6 convert_bitcast_fusion.1
  293.3 0.6 copy-done.10
  293.9 5.2 %convolution_bitcast_fusion = f32[128,64,128]{2,0,1:T(8,128)} fusion(bf16[1,64,128,128]{3,2,1,0:T(8,128)(2,1)S(1)} %copy-done, bf16[64,128,128]{2,1,0:T(8,128)(2,1)} %gather_fusion.7, pred[64]{0:T(512)(128)(4,1)S(1)} %copy-done.6), kind=kOutput, calls=%fused_computation.19 | convolution fusion | flops 269484032 | bytes 8388672 | tf_op jit(solution)/shard_map/nkc,kbc->nkb/dot_general | solution.py:97
  299.1 72.1 %all-gather.7.cloned.1.call-done = bf16[128,16384]{0,1:T(8,128)(2,1)} async-done(((bf16[128,512]{0,1:T(8,128)(2,1)}), bf16[128,16384]{0,1:T(8,128)(2,1)}) %all-gather.7.cloned.1.call-update) | async-done | bytes 4194320 | tf_op jit(solution)/shard_map/all_gather | solution.py:69
  371.2 6.5 %copy.125 = bf16[128,128,128]{2,0,1:T(8,128)(2,1)} copy(bf16[128,128,128]{0,2,1:T(8,128)(2,1)} %bitcast.107) | data formatting | bytes 8388608 | tf_op jit(solution)/shard_map/reshape | solution.py:28
  377.7 2.8 gather_fusion.3
  380.6 2.1 gather_fusion.4
  382.8 4.6 convert_bitcast_fusion
  387.4 0.6 copy-done.14
  387.9 6.1 %fusion.36 = bf16[128,32,128]{2,1,0:T(8,128)(2,1)S(1)} fusion(f32[128,64,128]{2,0,1:T(8,128)} %convolution_bitcast_fusion, s32[64]{0:T(128)S(1)} %copy-done.14), kind=kOutput, calls=%fused_computation.45 | convolution fusion | flops 403179520 | bytes 5243136 | tf_op jit(solution)/shard_map/nkb,kr->nrb/dot_general | solution.py:98
  394.0 0.5 reshape.232
  394.5 2.8 copy.138
  397.3 0.5 broadcast.484
  397.9 22.4 %reduce.15 = bf16[4096,128]{1,0:T(8,128)(2,1)S(1)} reduce(bf16[4096,1,128]{2,1,0:T(2,128)(2,1)S(1)} %bitcast.102, bf16[]{:T(256)} %broadcast.484), dimensions={1}, to_apply=%bitcast.95.reduce_sub_computation | reduce | bytes 2097154
  420.3 1.1 reshape.359
  421.4 7.0 %all-to-all-start.1 = ((bf16[32,2,8192]{2,1,0:T(2,128)(2,1)}), bf16[32,2,8192]{2,1,0:T(2,128)(2,1)S(1)}, u32[]{:S(2)}, u32[]{:S(2)}) async-start(bf16[32,2,8192]{2,1,0:T(2,128)(2,1)} %reshape.359), calls=%async_computation.1 | async-start | bytes 2097152 | tf_op jit(solution)/shard_map/all_to_all | solution.py:105
  428.4 2.4 convolution_bitcast_fusion.2
  430.8 4.1 fusion.39
  434.9 1.3 reshape.228
  436.2 5.0 copy.129
  441.2 23.4 %reduce.14 = bf16[4096,128]{1,0:T(8,128)(2,1)} reduce(bf16[4096,1,128]{2,1,0:T(2,128)(2,1)S(1)} %bitcast.103, bf16[]{:T(256)} %broadcast.484), dimensions={1}, to_apply=%bitcast.93.reduce_sub_computation | reduce | bytes 2097154
  464.6 2.1 reshape.357
  466.7 9.8 %all-to-all-start = ((bf16[32,2,8192]{2,1,0:T(2,128)(2,1)}), bf16[32,2,8192]{2,1,0:T(2,128)(2,1)}, u32[]{:S(2)}, u32[]{:S(2)}) async-start(bf16[32,2,8192]{2,1,0:T(2,128)(2,1)} %reshape.357), calls=%async_computation | async-start | bytes 2097152 | tf_op jit(solution)/shard_map/all_to_all | solution.py:104
  476.6 0.7 copy.185
  477.3 1.0 reshape.360
  478.6 0.7 copy.142
  479.3 22.0 %all-to-all-done = bf16[32,2,8192]{2,1,0:T(2,128)(2,1)} async-done(((bf16[32,2,8192]{2,1,0:T(2,128)(2,1)}), bf16[32,2,8192]{2,1,0:T(2,128)(2,1)}, u32[]{:S(2)}, u32[]{:S(2)}) %all-to-all-start) | async-done | bytes 1048608 | tf_op jit(solution)/shard_map/all_to_all | solution.py:104
  501.3 5.8 %reshape.358 = bf16[4096,1,128]{2,1,0:T(2,128)(2,1)} reshape(bf16[32,2,8192]{2,1,0:T(2,128)(2,1)} %all-to-all-done) | data formatting | bytes 2097152
  507.1 1.9 copy.147
  509.2 0.7 copy.141
  (84 shorter events, 2.5 us)
Async XLA Ops:
  7.2 177.9 %copy-start = (bf16[1,64,128,128]{3,2,1,0:T(8,128)(2,1)S(1)}, bf16[1,64,128,128]{3,2,1,0:T(8,128)(2,1)}, u32[]{:S(2)}) copy-start(bf16[1,64,128,128]{3,2,1,0:T(8,128)(2,1)} %param.16) | copy-start | bytes 6291460
  7.2 90.8 %all-gather.9.cloned.1.call-start = ((), (), s32[]{:S(2)}) async-start(), calls=%async_computation.6 | async-start | bytes 1081344 | tf_op jit(solution)/shard_map/all_gather | solution.py:46
  8.9 172.4 %all-gather.5.cloned.1.call-start = ((), (), s32[]{:S(2)}) async-start(), calls=%async_computation.4 | async-start | bytes 1081344 | tf_op jit(solution)/shard_map/all_gather | solution.py:45
  10.4 259.9 %all-gather.11.cloned.1.call-start = ((), (), s32[]{:S(2)}) async-start(), calls=%async_computation.7 | async-start | bytes 4325376 | tf_op jit(solution)/shard_map/all_gather | solution.py:88
  18.3 83.5 %copy-start.11 = (s32[64]{0:T(128)}, s32[64]{0:T(128)S(1)}, u32[]{:S(2)}) copy-start(s32[64]{0:T(128)S(1)} %get-tuple-element.20) | copy-start | bytes 772
  18.3 87.3 %copy-start.4 = (s32[64]{0:T(128)}, s32[64]{0:T(128)S(1)}, u32[]{:S(2)}) copy-start(s32[64]{0:T(128)S(1)} %get-tuple-element.33) | copy-start | bytes 772
  105.6 4.7 copy-start.9
  105.7 5.0 copy-start.3
  110.3 260.9 %all-gather.7.cloned.1.call-start = ((), (), s32[]{:S(2)}) async-start(), calls=%async_computation.5 | async-start | bytes 4325376 | tf_op jit(solution)/shard_map/all_gather | solution.py:69
  114.6 0.5 copy-start.13
  114.6 70.4 %copy-start.7 = (pred[64]{0:T(512)(128)(4,1)}, pred[64]{0:T(512)(128)(4,1)S(1)}, u32[]{:S(2)}) copy-start(pred[64]{0:T(512)(128)(4,1)S(1)} %get-tuple-element.38) | copy-start | bytes 196
  270.3 9.2 %copy-start.15 = (s32[64]{0:T(128)S(1)}, s32[64]{0:T(128)}, u32[]{:S(2)}) copy-start(s32[64]{0:T(128)} %get-tuple-element.14) | copy-start | bytes 772
  270.3 9.2 %copy-start.16 = (pred[4]{0:T(512)(128)(4,1)S(1)}, pred[4]{0:T(512)(128)(4,1)}, u32[]{:S(2)}) copy-start(pred[4]{0:T(512)(128)(4,1)} %get-tuple-element.15) | copy-start | bytes 16
  270.3 9.2 %copy-start.17 = (pred[4]{0:T(512)(128)(4,1)S(1)}, pred[4]{0:T(512)(128)(4,1)}, u32[]{:S(2)}) copy-start(pred[4]{0:T(512)(128)(4,1)} %get-tuple-element.17) | copy-start | bytes 16
  286.3 223.6 %reduce-scatter.3.cloned.1.call-start = ((), (), s32[]{:S(2)}) async-start(), calls=%async_computation.8 | async-start | bytes 2228224 | tf_op jit(solution)/shard_map/reduce_scatter | solution.py:110
  286.4 2.2 copy-start.6
  286.4 2.2 copy-start.8
  293.2 0.7 copy-start.10
  293.2 0.7 copy-start.5
  293.2 216.7 %reduce-scatter.5.cloned.1.call-start = ((), (), s32[]{:S(2)}) async-start(), calls=%async_computation.9 | async-start | bytes 2228224 | tf_op jit(solution)/shard_map/reduce_scatter | solution.py:113
  387.3 0.6 copy-start.14
  420.2 8.2 %copy-start.2 = (bf16[64,128,128]{2,1,0:T(8,128)(2,1)S(1)}, bf16[64,128,128]{2,1,0:T(8,128)(2,1)}, u32[]{:S(2)}) copy-start(bf16[64,128,128]{2,1,0:T(8,128)(2,1)} %gather_fusion.4) | copy-start | bytes 6291460
  421.4 45.4 %all-to-all-start.1 = ((bf16[32,2,8192]{2,1,0:T(2,128)(2,1)}), bf16[32,2,8192]{2,1,0:T(2,128)(2,1)S(1)}, u32[]{:S(2)}, u32[]{:S(2)}) async-start(bf16[32,2,8192]{2,1,0:T(2,128)(2,1)} %reshape.359), calls=%async_computation.1 | async-start | bytes 2097152 | tf_op jit(solution)/shard_map/all_to_all | solution.py:105
  428.4 2.4 copy-start.12
  466.7 34.6 %all-to-all-start = ((bf16[32,2,8192]{2,1,0:T(2,128)(2,1)}), bf16[32,2,8192]{2,1,0:T(2,128)(2,1)}, u32[]{:S(2)}, u32[]{:S(2)}) async-start(bf16[32,2,8192]{2,1,0:T(2,128)(2,1)} %reshape.357), calls=%async_computation | async-start | bytes 2097152 | tf_op jit(solution)/shard_map/all_to_all | solution.py:104
  507.1 2.8 copy-start.1
Sparse Core Ops, SparseCore 0:
  11.8 86.1 all-gather.8
  101.7 79.5 all-gather.4
  185.0 85.2 all-gather.10
  286.4 84.7 all-gather.6
  374.4 59.0 reduce-scatter.2
  436.8 61.4 reduce-scatter.4
where the time goes:
time: 525 us; the launch traced here: 517 us
  waiting for transfers between devices  321 us (61%)
  local copies, waits for them, and re-layouts  67 us (13%)
  other arithmetic  52.4 us (10%)
  matrix products  44.8 us (9%)
  starting transfers between devices  17.1 us (3%)
  between operations  14.8 us (3%)
    all_gather x1, waiting for transfers between devices, shards(): lax.all_gather(dh_owned, 'tensor', axis=1, tiled=True)  80.9 us
    all_gather x1, waiting for transfers between devices, shards(): lax.all_gather(cotangent, 'tensor', axis=1, tiled=True)  79.6 us
    all_gather x1, waiting for transfers between devices, shards(): lax.all_gather(hidden, 'tensor', axis=1, tiled=True)  72.1 us
    all_gather x1, waiting for transfers between devices, shards(): lax.all_gather(tokens, 'tensor', axis=1, tiled=True)  66.1 us
    unnamed x2, other arithmetic  45.8 us
    all_to_all x1, waiting for transfers between devices, shards(): lax.all_to_all(out_part, 'tensor', split_axis=2, concat_axis=0, tiled=True)  22 us
    unnamed x50, local copies, waits for them, and re-layouts  20.5 us
    reshape x2, local copies, waits for them, and re-layouts, picker(): shaped = segment.reshape(segment.shape[0], block_count, block)  12.9 us
  transfers between devices with their start and end apart: 8, of which 5 were waited for; matrix products, arithmetic and copies ran while one was open for 28% of the time, Pallas kernels for 0%

commit v1 on v0

--- a/solution.py
+++ b/solution.py
@@ -2,6 +2,27 @@
 import jax.numpy as jnp
 from jax import lax
 from jax.sharding import PartitionSpec as P
+
+
+def laid_out(blocks, dim):
+    shape = list(blocks.shape[1:])
+    shape[dim] *= blocks.shape[0]
+    return jnp.moveaxis(blocks, 0, dim).reshape(shape)
+
+
+def collected_by_bits(x, axis):
+    count, index = (lax.axis_size(axis), lax.axis_index(axis))
+    blocks, apart = (x[None], 1)
+    while apart < count:
+        other = lax.ppermute(blocks, axis, [(i, i ^ apart) for i in range(count)])
+        low = index & apart == 0
+        blocks = jnp.concatenate([jnp.where(low, blocks, other), jnp.where(low, other, blocks)])
+        apart *= 2
+    return blocks
+
+
+def gather_by_bits(value, axis, dim):
+    return laid_out(collected_by_bits(value, axis), dim)
 
 
 def kept_positions(marked, total):
@@ -42,7 +63,7 @@
     model_width = blocks_wide * block
     highest = lax.Precision.HIGHEST
     x_full, dy_full = (
-        lax.all_gather(tokens, "tensor", axis=1, tiled=True),
+        gather_by_bits(tokens, "tensor", 1),
         lax.all_gather(cotangent, "tensor", axis=1, tiled=True),
     )
     token_blocks = x_full.reshape(token_count, blocks_wide, block)

time: 525 us -> 459 us (0.87)
  waiting for transfers between devices: 321 us -> 240 us
  starting transfers between devices: 17.1 us -> 36 us
    all_gather x1 -> x0, waiting for transfers between devices: 66.1 us -> none  [shards(): lax.all_gather(tokens, 'tensor', axis=1, tiled=True)]
    all_gather x1, waiting for transfers between devices: 80.9 us -> 19.5 us  [shards(): lax.all_gather(dh_owned, 'tensor', axis=1, tiled=True)]
    ppermute x0 -> x5, waiting for transfers between devices: none -> 44.8 us  [collected_by_bits(): other = lax.ppermute(blocks, axis, [(i, i ^ apart) for i in range(count)])]
    ppermute x0 -> x5, starting transfers between devices: none -> 18.9 us  [collected_by_bits(): other = lax.ppermute(blocks, axis, [(i, i ^ apart) for i in range(count)])]
    unnamed x50 -> x51, local copies, waits for them, and re-layouts: 20.5 us -> 18.5 us
  transfers between devices with their start and end apart: 8 -> 12, of which waited for: 5 -> 9; matrix products, arithmetic and copies ran while one was open for 28% -> 29% of each run, Pallas kernels for 0% -> 0%
where the time goes in v1:
time: 459 us; the launch traced here: 451 us
  waiting for transfers between devices  240 us (52%)
  local copies, waits for them, and re-layouts  62.9 us (14%)
  other arithmetic  52.7 us (11%)
  matrix products  44.9 us (10%)
  starting transfers between devices  36 us (8%)
  between operations  14.6 us (3%)
    all_gather x1, waiting for transfers between devices, shards(): lax.all_gather(cotangent, 'tensor', axis=1, tiled=True)  81.1 us
    all_gather x1, waiting for transfers between devices, shards(): lax.all_gather(hidden, 'tensor', axis=1, tiled=True)  72.4 us
    unnamed x2, other arithmetic  45.8 us
    ppermute x5, waiting for transfers between devices, collected_by_bits(): other = lax.ppermute(blocks, axis, [(i, i ^ apart) for i in range(count)])  44.8 us
    all_to_all x1, waiting for transfers between devices, shards(): lax.all_to_all(out_part, 'tensor', split_axis=2, concat_axis=0, tiled=True)  22 us
    all_gather x1, waiting for transfers between devices, shards(): lax.all_gather(dh_owned, 'tensor', axis=1, tiled=True)  19.5 us
    ppermute x5, starting transfers between devices, collected_by_bits(): other = lax.ppermute(blocks, axis, [(i, i ^ apart) for i in range(count)])  18.9 us
    unnamed x51, local copies, waits for them, and re-layouts  18.5 us
  transfers between devices with their start and end apart: 12, of which 9 were waited for; matrix products, arithmetic and copies ran while one was open for 29% of the time, Pallas kernels for 0%

profile of v1, /device:TPU:2, one launch (start us, length us, event | category | flops | bytes accessed | tf_op | source)
XLA Modules:
  0.0 451.1 jit_solution(6329616484222681552)
XLA Ops:
  7.2 1.6 copy.123
  8.9 0.7 fusion.58
  9.7 0.7 fusion.72
  10.4 0.8 copy.110
  11.7 0.8 select_reduce_fusion
  12.5 0.7 multiply_add_fusion
  13.2 1.0 scatter_custom_fusion
  14.2 0.6 gather_fusion
  15.8 1.0 scatter_custom_fusion.1
  16.8 81.1 %all-gather.6.cloned.1.call-done = bf16[128,4096]{0,1:T(8,128)(2,1)} async-done(((bf16[128,128]{0,1:T(8,128)(2,1)}), bf16[128,4096]{0,1:T(8,128)(2,1)}) %all-gather.6.cloned.1.call-update) | async-done | bytes 1048592 | tf_op jit(solution)/shard_map/all_gather | solution.py:67
  98.0 1.6 copy.124
  99.6 2.1 gather_fusion.5
  101.8 3.8 convolution_bitcast_fusion.1
  105.6 3.8 fusion.48
  109.4 0.8 copy.139
  110.3 3.2 collective-permute-start
  114.1 1.0 scatter_custom_fusion.2
  115.1 1.4 collective-permute-done
  116.5 3.5 collective-permute-start.1
  120.1 0.6 gather_fusion.1
  120.7 3.5 collective-permute-done.1
  124.2 2.6 collective-permute-start.2
  126.8 0.5 compare_and_fusion
  127.3 4.6 %collective-permute-done.2 = bf16[4,128,128]{2,1,0:T(8,128)(2,1)S(1)} collective-permute-done((bf16[4,128,128]{2,1,0:T(8,128)(2,1)S(1)}, bf16[4,128,128]{2,1,0:T(8,128)(2,1)S(1)}, u32[]{:S(2)}, u32[]{:S(2)}) %collective-permute-start.2) | collective-permute-done | bytes 131104 | tf_op jit(solution)/shard_map/ppermute | solution.py:17
  132.0 4.0 collective-permute-start.3
  136.1 21.3 %collective-permute-done.3 = bf16[8,128,128]{2,1,0:T(8,128)(2,1)S(1)} collective-permute-done((bf16[8,128,128]{2,1,0:T(8,128)(2,1)S(1)}, bf16[8,128,128]{2,1,0:T(8,128)(2,1)S(1)}, u32[]{:S(2)}, u32[]{:S(2)}) %collective-permute-start.3) | collective-permute-done | bytes 262176 | tf_op jit(solution)/shard_map/ppermute | solution.py:17
  157.5 5.6 %collective-permute-start.4 = (bf16[16,128,128]{2,1,0:T(8,128)(2,1)S(1)}, bf16[16,128,128]{2,1,0:T(8,128)(2,1)S(1)}, u32[]{:S(2)}, u32[]{:S(2)}) collective-permute-start(bf16[16,128,128]{2,1,0:T(8,128)(2,1)S(1)} %pad_maximum_fusion), channel_id=1, source_target_pairs={{0,16},{1,17},{2,18},{3,19},{4,20},{5,21},{6,22},{7,23},{8,24},{9,... | collective-permute-start | bytes 1572872 | tf_op jit(solution)/shard_map/ppermute | solution.py:17
  164.2 13.9 %collective-permute-done.4 = bf16[16,128,128]{2,1,0:T(8,128)(2,1)S(1)} collective-permute-done((bf16[16,128,128]{2,1,0:T(8,128)(2,1)S(1)}, bf16[16,128,128]{2,1,0:T(8,128)(2,1)S(1)}, u32[]{:S(2)}, u32[]{:S(2)}) %collective-permute-start.4) | collective-permute-done | bytes 524320 | tf_op jit(solution)/shard_map/ppermute | solution.py:17
  178.3 2.2 gather_fusion.2
  180.5 4.4 convolution_bitcast_fusion.3
  184.9 19.5 %all-gather.8.cloned.1.call-done = bf16[128,16384]{0,1:T(8,128)(2,1)} async-done(((bf16[128,512]{0,1:T(8,128)(2,1)}), bf16[128,16384]{0,1:T(8,128)(2,1)}) %all-gather.8.cloned.1.call-update) | async-done | bytes 4194320 | tf_op jit(solution)/shard_map/all_gather | solution.py:109
  204.4 6.4 %copy.127 = bf16[128,128,128]{2,0,1:T(8,128)(2,1)} copy(bf16[128,128,128]{0,2,1:T(8,128)(2,1)} %bitcast.113) | data formatting | bytes 8388608 | tf_op jit(solution)/shard_map/reshape | solution.py:49
  210.8 2.8 gather_fusion.6
  213.6 6.0 %fusion.54 = (bf16[128,4,128]{2,1,0:T(4,128)(2,1)S(1)}, bf16[128,4,128]{2,1,0:T(4,128)(2,1)S(1)}, bf16[128,4,128]{2,1,0:T(4,128)(2,1)S(1)}) fusion(f32[128,4,128]{2,1,0:T(4,128)S(1)} %reshape.230, bf16[4,128,128]{2,1,0:T(8,128)(2,1)S(1)} %gather_fusion.6, pred[4]{0:T(512)(128)(4,1)S(1)} %copy-done.18, pred[4]{0:T(512)(128)(4,1)S(1)} %copy-done.17, ...), kind=kOutput, calls=%fused_computation.59 | convolution fusion | flops 51511552 | bytes 4981000 | tf_op jit(solution)/shard_map/nkc,ks->nsc/dot_general | solution.py:78
  219.7 0.8 copy.138
  220.6 2.2 gather_fusion.7
  222.8 4.6 %convert_bitcast_fusion.1 = bf16[1,64,128,128]{3,2,1,0:T(8,128)(2,1)} fusion(bf16[64,128,128]{2,1,0:T(8,128)(2,1)} %gather_fusion.2, pred[64]{0:T(512)(128)(4,1)S(1)} %copy-done.9, bf16[64,128,128]{2,1,0:T(8,128)(2,1)} %gather_fusion.7, pred[64]{0:T(512)(128)(4,1)S(1)} %copy-done.7), kind=kOutput, calls=%fused_computation.38 | convolution fusion | flops 271581184 | bytes 6291584 | tf_op jit(solution)/shard_map/nkb,nkc->kbc/dot_general | solution.py:121
  227.4 0.6 copy-done.11
  228.0 5.2 %convolution_bitcast_fusion = f32[128,64,128]{2,0,1:T(8,128)} fusion(bf16[1,64,128,128]{3,2,1,0:T(8,128)(2,1)S(1)} %copy-done, bf16[64,128,128]{2,1,0:T(8,128)(2,1)} %gather_fusion.7, pred[64]{0:T(512)(128)(4,1)S(1)} %copy-done.7), kind=kOutput, calls=%fused_computation.19 | convolution fusion | flops 269484032 | bytes 8388672 | tf_op jit(solution)/shard_map/nkc,kbc->nkb/dot_general | solution.py:118
  233.2 72.4 %all-gather.4.cloned.1.call-done = bf16[128,16384]{0,1:T(8,128)(2,1)} async-done(((bf16[128,512]{0,1:T(8,128)(2,1)}), bf16[128,16384]{0,1:T(8,128)(2,1)}) %all-gather.4.cloned.1.call-update) | async-done | bytes 4194320 | tf_op jit(solution)/shard_map/all_gather | solution.py:90
  305.6 6.5 %copy.118 = bf16[128,128,128]{2,0,1:T(8,128)(2,1)} copy(bf16[128,128,128]{0,2,1:T(8,128)(2,1)} %bitcast.114) | data formatting | bytes 8388608 | tf_op jit(solution)/shard_map/reshape | solution.py:49
  312.1 2.8 gather_fusion.3
  315.1 2.1 gather_fusion.4
  317.2 4.6 %convert_bitcast_fusion = bf16[1,64,128,128]{3,2,1,0:T(8,128)(2,1)} fusion(bf16[64,128,128]{2,1,0:T(8,128)(2,1)} %gather_fusion.4, pred[64]{0:T(512)(128)(4,1)S(1)} %get-tuple-element.42, bf16[64,128,128]{2,1,0:T(8,128)(2,1)} %gather_fusion.5, pred[64]{0:T(512)(128)(4,1)S(1)} %get-tuple-element.19), kind=kOutput, calls=%fused_computation.37 | convolution fusion | flops 271581184 | bytes 6291584 | tf_op jit(solution)/shard_map/nkb,nkc->kbc/dot_general | solution.py:99
  321.8 0.6 copy-done.15
  322.4 6.1 %fusion.36 = bf16[128,32,128]{2,1,0:T(8,128)(2,1)S(1)} fusion(f32[128,64,128]{2,0,1:T(8,128)} %convolution_bitcast_fusion, s32[64]{0:T(128)S(1)} %copy-done.15), kind=kOutput, calls=%fused_computation.45 | convolution fusion | flops 403179520 | bytes 5243136 | tf_op jit(solution)/shard_map/nkb,kr->nrb/dot_general | solution.py:119
  329.0 2.8 copy.131
  332.3 22.4 %reduce.15 = bf16[4096,128]{1,0:T(8,128)(2,1)S(1)} reduce(bf16[4096,1,128]{2,1,0:T(2,128)(2,1)S(1)} %bitcast.109, bf16[]{:T(256)} %broadcast.484), dimensions={1}, to_apply=%bitcast.99.reduce_sub_computation | reduce | bytes 2097154
  354.7 1.1 reshape.355
  355.8 7.0 %all-to-all-start.1 = ((bf16[32,2,8192]{2,1,0:T(2,128)(2,1)}), bf16[32,2,8192]{2,1,0:T(2,128)(2,1)S(1)}, u32[]{:S(2)}, u32[]{:S(2)}) async-start(bf16[32,2,8192]{2,1,0:T(2,128)(2,1)} %reshape.355), calls=%async_computation.1 | async-start | bytes 2097152 | tf_op jit(solution)/shard_map/all_to_all | solution.py:126
  362.9 2.4 convolution_bitcast_fusion.2
  365.3 4.1 fusion.39
  369.3 1.3 reshape.224
  370.6 5.0 %copy.122 = bf16[1,128,4096]{1,0,2:T(2,128)(2,1)S(1)} copy(bf16[1,128,4096]{2,1,0:T(8,128)(2,1)} %reshape.224) | data formatting | bytes 2097152 | tf_op jit(solution)/shard_map/reshape | solution.py:97
  375.7 23.4 %reduce.14 = bf16[4096,128]{1,0:T(8,128)(2,1)} reduce(bf16[4096,1,128]{2,1,0:T(2,128)(2,1)S(1)} %bitcast.110, bf16[]{:T(256)} %broadcast.484), dimensions={1}, to_apply=%bitcast.97.reduce_sub_computation | reduce | bytes 2097154
  399.0 2.1 reshape.353
  401.2 9.8 %all-to-all-start = ((bf16[32,2,8192]{2,1,0:T(2,128)(2,1)}), bf16[32,2,8192]{2,1,0:T(2,128)(2,1)}, u32[]{:S(2)}, u32[]{:S(2)}) async-start(bf16[32,2,8192]{2,1,0:T(2,128)(2,1)} %reshape.353), calls=%async_computation | async-start | bytes 2097152 | tf_op jit(solution)/shard_map/all_to_all | solution.py:125
  411.0 0.7 copy.178
  411.7 1.0 reshape.356
  413.1 0.7 copy.135
  413.8 22.0 %all-to-all-done = bf16[32,2,8192]{2,1,0:T(2,128)(2,1)} async-done(((bf16[32,2,8192]{2,1,0:T(2,128)(2,1)}), bf16[32,2,8192]{2,1,0:T(2,128)(2,1)}, u32[]{:S(2)}, u32[]{:S(2)}) %all-to-all-start) | async-done | bytes 1048608 | tf_op jit(solution)/shard_map/all_to_all | solution.py:125
  435.8 5.7 %reshape.354 = bf16[4096,1,128]{2,1,0:T(2,128)(2,1)} reshape(bf16[32,2,8192]{2,1,0:T(2,128)(2,1)} %all-to-all-done) | data formatting | bytes 2097152
  441.5 1.9 copy.140
  443.6 0.7 copy.134
  (101 shorter events, 5.6 us)
Async XLA Ops:
  7.2 173.3 %copy-start = (bf16[1,64,128,128]{3,2,1,0:T(8,128)(2,1)S(1)}, bf16[1,64,128,128]{3,2,1,0:T(8,128)(2,1)}, u32[]{:S(2)}) copy-start(bf16[1,64,128,128]{3,2,1,0:T(8,128)(2,1)} %param.16) | copy-start | bytes 6291460
  7.2 90.8 %all-gather.6.cloned.1.call-start = ((), (), s32[]{:S(2)}) async-start(), calls=%async_computation.5 | async-start | bytes 1081344 | tf_op jit(solution)/shard_map/all_gather | solution.py:67
  8.9 195.6 %all-gather.8.cloned.1.call-start = ((), (), s32[]{:S(2)}) async-start(), calls=%async_computation.6 | async-start | bytes 4325376 | tf_op jit(solution)/shard_map/all_gather | solution.py:109
  16.8 85.0 %copy-start.12 = (s32[64]{0:T(128)}, s32[64]{0:T(128)S(1)}, u32[]{:S(2)}) copy-start(s32[64]{0:T(128)S(1)} %get-tuple-element.20) | copy-start | bytes 772
  16.8 88.8 %copy-start.5 = (s32[64]{0:T(128)}, s32[64]{0:T(128)S(1)}, u32[]{:S(2)}) copy-start(s32[64]{0:T(128)S(1)} %get-tuple-element.43) | copy-start | bytes 772
  105.6 4.7 %copy-start.4 = (bf16[128,128]{1,0:T(8,128)(2,1)S(1)}, bf16[128,128]{1,0:T(8,128)(2,1)}, u32[]{:S(2)}) copy-start(bf16[128,128]{1,0:T(8,128)(2,1)} %param.14) | copy-start | bytes 98308
  105.6 7.9 %copy-start.10 = (s32[32,4]{0,1:T(4,128)S(1)}, s32[32,4]{0,1:T(4,128)}, u32[]{:S(2)}) copy-start(s32[32,4]{0,1:T(4,128)} %param.17) | copy-start | bytes 1540
  105.6 8.3 %copy-start.3 = (bf16[128,512]{1,0:T(8,128)(2,1)S(1)}, bf16[128,512]{1,0:T(8,128)(2,1)}, u32[]{:S(2)}) copy-start(bf16[128,512]{1,0:T(8,128)(2,1)} %param.15) | copy-start | bytes 393220
  110.3 195.4 %all-gather.4.cloned.1.call-start = ((), (), s32[]{:S(2)}) async-start(), calls=%async_computation.4 | async-start | bytes 4325376 | tf_op jit(solution)/shard_map/all_gather | solution.py:90
  110.3 6.2 %collective-permute-start = (bf16[1,128,128]{2,1,0:T(8,128)(2,1)S(1)}, bf16[1,128,128]{2,1,0:T(8,128)(2,1)S(1)}, u32[]{:S(2)}, u32[]{:S(2)}) collective-permute-start(bf16[1,128,128]{2,1,0:T(8,128)(2,1)S(1)} %bitcast.120), channel_id=1, source_target_pairs={{0,1},{1,0},{2,3},{3,2},{4,5},{5,4},{6,7},{7,6},{8,9},{9,8},{10,11... | collective-permute-start | bytes 98312 | tf_op jit(solution)/shard_map/ppermute | solution.py:17
  116.5 7.7 %collective-permute-start.1 = (bf16[2,128,128]{2,1,0:T(8,128)(2,1)S(1)}, bf16[2,128,128]{2,1,0:T(8,128)(2,1)S(1)}, u32[]{:S(2)}, u32[]{:S(2)}) collective-permute-start(bf16[2,128,128]{2,1,0:T(8,128)(2,1)S(1)} %pad_maximum_fusion.3), channel_id=1, source_target_pairs={{0,2},{1,3},{2,0},{3,1},{4,6},{5,7},{6,4},{7,5},{8,10},{9,11},{10,... | collective-permute-start | bytes 196616 | tf_op jit(solution)/shard_map/ppermute | solution.py:17
  124.2 7.8 %collective-permute-start.2 = (bf16[4,128,128]{2,1,0:T(8,128)(2,1)S(1)}, bf16[4,128,128]{2,1,0:T(8,128)(2,1)S(1)}, u32[]{:S(2)}, u32[]{:S(2)}) collective-permute-start(bf16[4,128,128]{2,1,0:T(8,128)(2,1)S(1)} %pad_maximum_fusion.2), channel_id=1, source_target_pairs={{0,4},{1,5},{2,6},{3,7},{4,0},{5,1},{6,2},{7,3},{8,12},{9,13},{10,... | collective-permute-start | bytes 393224 | tf_op jit(solution)/shard_map/ppermute | solution.py:17
  127.3 8.7 %copy-start.14 = (s32[64]{0:T(128)}, s32[64]{0:T(128)S(1)}, u32[]{:S(2)}) copy-start(s32[64]{0:T(128)S(1)} %get-tuple-element.49) | copy-start | bytes 772
  127.3 53.1 %copy-start.8 = (pred[64]{0:T(512)(128)(4,1)}, pred[64]{0:T(512)(128)(4,1)S(1)}, u32[]{:S(2)}) copy-start(pred[64]{0:T(512)(128)(4,1)S(1)} %get-tuple-element.48) | copy-start | bytes 196
  132.0 25.4 %collective-permute-start.3 = (bf16[8,128,128]{2,1,0:T(8,128)(2,1)S(1)}, bf16[8,128,128]{2,1,0:T(8,128)(2,1)S(1)}, u32[]{:S(2)}, u32[]{:S(2)}) collective-permute-start(bf16[8,128,128]{2,1,0:T(8,128)(2,1)S(1)} %pad_maximum_fusion.1), channel_id=1, source_target_pairs={{0,8},{1,9},{2,10},{3,11},{4,12},{5,13},{6,14},{7,15},{8,0},{9,1},... | collective-permute-start | bytes 786440 | tf_op jit(solution)/shard_map/ppermute | solution.py:17
  157.5 20.6 %collective-permute-start.4 = (bf16[16,128,128]{2,1,0:T(8,128)(2,1)S(1)}, bf16[16,128,128]{2,1,0:T(8,128)(2,1)S(1)}, u32[]{:S(2)}, u32[]{:S(2)}) collective-permute-start(bf16[16,128,128]{2,1,0:T(8,128)(2,1)S(1)} %pad_maximum_fusion), channel_id=1, source_target_pairs={{0,16},{1,17},{2,18},{3,19},{4,20},{5,21},{6,22},{7,23},{8,24},{9,... | collective-permute-start | bytes 1572872 | tf_op jit(solution)/shard_map/ppermute | solution.py:17
  204.4 9.2 %copy-start.16 = (s32[64]{0:T(128)S(1)}, s32[64]{0:T(128)}, u32[]{:S(2)}) copy-start(s32[64]{0:T(128)} %get-tuple-element.14) | copy-start | bytes 772
  204.4 9.2 %copy-start.17 = (pred[4]{0:T(512)(128)(4,1)S(1)}, pred[4]{0:T(512)(128)(4,1)}, u32[]{:S(2)}) copy-start(pred[4]{0:T(512)(128)(4,1)} %get-tuple-element.15) | copy-start | bytes 16
  204.4 9.2 %copy-start.18 = (pred[4]{0:T(512)(128)(4,1)S(1)}, pred[4]{0:T(512)(128)(4,1)}, u32[]{:S(2)}) copy-start(pred[4]{0:T(512)(128)(4,1)} %get-tuple-element.17) | copy-start | bytes 16
  220.5 223.8 %reduce-scatter.3.cloned.1.call-start = ((), (), s32[]{:S(2)}) async-start(), calls=%async_computation.7 | async-start | bytes 2228224 | tf_op jit(solution)/shard_map/reduce_scatter | solution.py:131
  220.6 2.2 copy-start.7
  220.6 2.2 copy-start.9
  227.3 0.7 copy-start.11
  227.3 0.7 copy-start.6
  227.3 217.0 %reduce-scatter.5.cloned.1.call-start = ((), (), s32[]{:S(2)}) async-start(), calls=%async_computation.8 | async-start | bytes 2228224 | tf_op jit(solution)/shard_map/reduce_scatter | solution.py:134
  321.8 0.6 copy-start.15
  354.7 8.2 %copy-start.2 = (bf16[64,128,128]{2,1,0:T(8,128)(2,1)S(1)}, bf16[64,128,128]{2,1,0:T(8,128)(2,1)}, u32[]{:S(2)}) copy-start(bf16[64,128,128]{2,1,0:T(8,128)(2,1)} %gather_fusion.4) | copy-start | bytes 6291460
  355.8 45.4 %all-to-all-start.1 = ((bf16[32,2,8192]{2,1,0:T(2,128)(2,1)}), bf16[32,2,8192]{2,1,0:T(2,128)(2,1)S(1)}, u32[]{:S(2)}, u32[]{:S(2)}) async-start(bf16[32,2,8192]{2,1,0:T(2,128)(2,1)} %reshape.355), calls=%async_computation.1 | async-start | bytes 2097152 | tf_op jit(solution)/shard_map/all_to_all | solution.py:126
  362.9 2.4 copy-start.13
  401.2 34.6 %all-to-all-start = ((bf16[32,2,8192]{2,1,0:T(2,128)(2,1)}), bf16[32,2,8192]{2,1,0:T(2,128)(2,1)}, u32[]{:S(2)}, u32[]{:S(2)}) async-start(bf16[32,2,8192]{2,1,0:T(2,128)(2,1)} %reshape.353), calls=%async_computation | async-start | bytes 2097152 | tf_op jit(solution)/shard_map/all_to_all | solution.py:125
  441.5 2.8 copy-start.1
Sparse Core Ops, SparseCore 0:
  11.8 86.1 all-gather.5
  110.4 94.0 all-gather.7
  220.6 84.9 all-gather.3
  308.9 59.0 reduce-scatter.2
  371.2 61.5 reduce-scatter.4
